TPU v7x, 32 devices: a whole 2x2x4 slice. The times are simulated.
32 devices in a mesh: rep: 4 (over y, x), shard: 8 (over z, core).
Axes of the slice: x: 2, y: 2, z: 4, core: 2. Of those that a mesh axis runs over, the one named last changes fastest.
Arguments:
- tokens: bfloat16 [224, 144, 768], P(('rep', 'shard')), may hold values from -6 to 6
- out_grad: bfloat16 [224, 144, 768], P(('rep', 'shard')), may hold values from -6 to 6
- window_count: int32 [32], P(('rep', 'shard')), may hold values from 1 to 7, as said below
- qkv_weight: float32 [768, 2304], P('shard'), may hold values from -0.21875 to 0.21875
- qkv_first: float32 [768, 2304], P('shard')
- qkv_second: float32 [768, 2304], P('shard'), as said below
- output_weight: float32 [768, 768], P('shard'), may hold values from -0.875 to 0.875
- output_first: float32 [768, 768], P('shard'), may hold values from -320 to 320
- output_second: float32 [768, 768], P('shard'), may hold values from 1935.36 to 7741.44
- up_weight: float32 [768, 3072], P('shard'), may hold values from -0.21875 to 0.21875
- up_first: float32 [768, 3072], P('shard'), may hold values from -256 to 256
- up_second: float32 [768, 3072], P('shard'), may hold values from 1064.448 to 4193.28
- down_weight: float32 [3072, 768], P('shard'), may hold values from -0.109375 to 0.109375
- down_first: float32 [3072, 768], P('shard'), may hold values from -448 to 448
- down_second: float32 [3072, 768], P('shard'), may hold values from 3548.16 to 13870.08
- vectors: float32 [12, 768], P(None, 'shard')
- vector_first: float32 [12, 768], P(None, 'shard')
- vector_second: float32 [12, 768], P(None, 'shard'), as said below
- bias_table: float32 [536, 24], P('shard'), may hold values from -4 to 4
- table_first: float32 [536, 24], P('shard'), may hold values from -320 to 320
- table_second: float32 [536, 24], P('shard'), may hold values from 1935.36 to 7741.44
Outputs:
- layer_out: bfloat16 [224, 144, 768], P(('rep', 'shard'))
- input_grad: float32 [224, 144, 768], P(('rep', 'shard'))
- qkv_new: float32 [768, 2304], P('shard')
- qkv_moment: float32 [768, 2304], P('shard')
- qkv_square: float32 [768, 2304], P('shard')
- qkv_copy: bfloat16 [768, 2304], P('shard')
- output_new: float32 [768, 768], P('shard')
- output_moment: float32 [768, 768], P('shard')
- output_square: float32 [768, 768], P('shard')
- output_copy: bfloat16 [768, 768], P('shard')
- up_new: float32 [768, 3072], P('shard')
- up_moment: float32 [768, 3072], P('shard')
- up_square: float32 [768, 3072], P('shard')
- up_copy: bfloat16 [768, 3072], P('shard')
- down_new: float32 [3072, 768], P('shard')
- down_moment: float32 [3072, 768], P('shard')
- down_square: float32 [3072, 768], P('shard')
- down_copy: bfloat16 [3072, 768], P('shard')
- vector_new: float32 [12, 768], P(None, 'shard')
- vector_moment: float32 [12, 768], P(None, 'shard')
- vector_square: float32 [12, 768], P(None, 'shard')
- table_new: float32 [536, 24], P('shard')
- table_moment: float32 [536, 24], P('shard')
- table_square: float32 [536, 24], P('shard')
Inputs may be any that keep to these rules, and one draw needn't show every extreme that they name: `window_count`: some device holds 7 windows and some other holds 1 in every draw; a device's live windows are its first slots. `qkv_second`: Positive. `vector_second`: Positive.
All inputs are finite; a program needn't handle non-finite values.
Results may differ from a plain program's by a relative error of at most 0.012.
The roundings to bfloat16 on the way count: a program that leaves them out, or rounds other values in their place, can miss the bound.
Values may be sent and summed in bfloat16 or wider, within the bound.
A program may use at most 256 MiB of HBM per device.

v0:
```python
import functools
import math

import jax
import jax.numpy as jnp
import numpy as np
from jax import lax
from jax.experimental import pallas as pl
from jax.experimental.pallas import tpu as pltpu
from jax.sharding import PartitionSpec as P

C = 768
HEADS = 24
MLP = 3072
WIN = 12
STEP = 5
HEAD_DIM = 32
SPAN = 2 * WIN - 1
TOK = WIN * WIN
TAB_ROWS = 536
ROWS = 1024
GROUPS = 3
GCOLS = 256
GHEADS = 8
PACK = GHEADS * TOK
TAB_LANES = 640
TILES = 3
TILE = MLP // TILES
SUB = 512
LINE = 384
MIB = 1 << 20

beta_one = 0.5
beta_two = 0.6
weight_decay = 0.05
adam_eps = 1e-08
norm_eps = 1e-05
step_rates = (0.04, 0.15, 0.04, 0.02, 0.2, 1.0)
low = jnp.bfloat16
full = jnp.float32
NT = (((1,), (1,)), ((), ()))


def dot(a, b):
    return jnp.dot(a, b, preferred_element_type=full)


def dot_nt(a, b):
    return lax.dot_general(a, b, NT, preferred_element_type=full)


def line_matrix():
    out = np.zeros((TAB_LANES, LINE), np.float32)
    col = np.arange(SPAN * WIN)
    out[(col // WIN) * SPAN + col % WIN + WIN - 1, col] = 1.0
    return out


def head_masks():
    lane = np.arange(GCOLS) // HEAD_DIM
    one = (lane[None, :] == np.arange(GHEADS)[:, None]).astype(np.float32)
    return np.broadcast_to(one[:, None, :], (GHEADS, 16, GCOLS))


def norm_parts(z):
    mean = jnp.sum(z, -1, keepdims=True) * (1.0 / C)
    center = z - mean
    spread = jnp.sum(center * center, -1, keepdims=True) * (1.0 / C)
    scale = lax.rsqrt(spread + norm_eps)
    return center * scale, scale


def norm_back(xhat, scale, dn, gain):
    g = dn * gain
    m1 = jnp.sum(g, -1, keepdims=True) * (1.0 / C)
    m2 = jnp.sum(g * xhat, -1, keepdims=True) * (1.0 / C)
    return scale * (g - m1 - xhat * m2)


def diag(x, mask_ref):
    head = x[0:128].reshape(8, 16, GCOLS)
    tail = x[128:144]
    parts = []
    for h in range(GHEADS):
        parts.append((head * mask_ref[h][None]).reshape(128, GCOLS))
    for h in range(GHEADS):
        parts.append(tail * mask_ref[h])
    return jnp.concatenate(parts, 0)


def undiag(xt, m, mask_ref):
    main = []
    for h in range(0, GHEADS, 2):
        r = dot(xt[h * HEAD_DIM : (h + 2) * HEAD_DIM], m[:, h * 128 : (h + 2) * 128])
        main.append(r[0:HEAD_DIM, 0:128])
        main.append(r[HEAD_DIM : 2 * HEAD_DIM, 128:256])
    main = jnp.concatenate(main, 0)
    rest = dot(xt, m[:, GHEADS * 128 :])
    rest_t = rest.T.reshape(GHEADS, 16, GCOLS)
    keep = mask_ref[...].astype(full)
    return jnp.concatenate([main.T, jnp.sum(rest_t * keep, 0)], 0)


def flat(x):
    return x.reshape(x.shape[0] * x.shape[1], x.shape[2])


def blocks(x, owners):
    return x.reshape(owners, x.shape[0] // owners, x.shape[1])


def hidden_place(t, s):
    at = (MLP // GHEADS) * s + 128 * t
    return 8 + at // C, at % C


def unpack_small(small_ref, vec_ref):
    owners = small_ref.shape[0]
    width = C // owners
    count = TAB_ROWS // owners
    vec = jnp.zeros((16, C), full)
    tab = jnp.zeros((HEADS, TAB_LANES), full)
    lane = lax.broadcasted_iota(jnp.int32, (16, 128), 1)
    lane_tab = lax.broadcasted_iota(jnp.int32, (HEADS, 128), 1)
    for s in range(owners):
        piece = small_ref[s].astype(full)
        part = jnp.where(lane < width, piece[0:16], 0.0)
        part = jnp.concatenate([part, jnp.zeros((16, C - 128), full)], 1)
        vec = vec + (pltpu.roll(part, width * s, 1) if s else part)
        part = jnp.where(lane_tab < count, piece[16 : 16 + HEADS], 0.0)
        part = jnp.concatenate([part, jnp.zeros((HEADS, TAB_LANES - 128), full)], 1)
        tab = tab + (pltpu.roll(part, count * s, 1) if s else part)
    vec_ref[...] = vec
    return tab


def pack_small(vec, tab, out_ref):
    owners = out_ref.shape[0]
    width = C // owners
    count = TAB_ROWS // owners
    for s in range(owners):
        out_ref[s, 0:16, :] = (pltpu.roll(vec, C - width * s, 1) if s else vec)[:, 0:128]
        out_ref[s, 16:40, :] = (pltpu.roll(tab, TAB_LANES - count * s, 1) if s else tab)[:, 0:128]


def spread_table(tab, line_ref, tmp_ref):
    def column(cj, carry):
        shifted = pltpu.roll(tab, cj, 1)
        line = dot(shifted.astype(low), line_ref[...])
        for rj in range(WIN):
            cut = (WIN - 1 - rj) * WIN
            part = pltpu.roll(line, LINE - cut, 1) if cut else line
            row = pl.multiple_of((rj * WIN + cj) * HEADS, 8)
            tmp_ref[0, pl.ds(row, HEADS), :] = part[:, 0:128]
            tmp_ref[1, pl.ds(row, HEADS), :] = part[:, 128:256]
        return carry

    lax.fori_loop(0, WIN, column, 0)


def place_bias(tmp_ref, bias_ref):
    lane = lax.broadcasted_iota(jnp.int32, (TOK, 128), 1)
    for g in range(GROUPS):
        rest = jnp.zeros((TOK, 128), full)
        for h in range(GHEADS):
            at = pl.ds(g * GHEADS + h, TOK, stride=HEADS)
            bias_ref[g, :, h * 128 : (h + 1) * 128] = tmp_ref[0, at, :]
            piece = tmp_ref[1, at, :]
            piece = pltpu.roll(piece, 16 * h, 1) if h else piece
            rest = jnp.where((lane >= 16 * h) & (lane < 16 * h + 16), piece, rest)
        bias_ref[g, :, GHEADS * 128 :] = rest


def table_grad(line_ref, tmp_ref, bias_ref):
    lane = lax.broadcasted_iota(jnp.int32, (TOK, 128), 1)
    for g in range(GROUPS):
        rest = bias_ref[g, :, GHEADS * 128 :]
        for h in range(GHEADS):
            at = pl.ds(g * GHEADS + h, TOK, stride=HEADS)
            tmp_ref[0, at, :] = bias_ref[g, :, h * 128 : (h + 1) * 128]
            piece = pltpu.roll(rest, 128 - 16 * h, 1) if h else rest
            tmp_ref[1, at, :] = jnp.where(lane < 16, piece, 0.0)

    def column(cj, total):
        line = jnp.zeros((HEADS, LINE), full)
        for rj in range(WIN):
            cut = (WIN - 1 - rj) * WIN
            row = pl.multiple_of((rj * WIN + cj) * HEADS, 8)
            part = jnp.concatenate([tmp_ref[0, pl.ds(row, HEADS), :], tmp_ref[1, pl.ds(row, HEADS), :], jnp.zeros((HEADS, 128), full)], 1)
            line = line + (pltpu.roll(part, cut, 1) if cut else part)
        high = line.astype(low)
        rest = (line - high.astype(full)).astype(low)
        spread = dot_nt(high, line_ref[...]) + dot_nt(rest, line_ref[...])
        return total + pltpu.roll(spread, TAB_LANES - cj, 1)

    return lax.fori_loop(0, WIN, column, jnp.zeros((HEADS, TAB_LANES), full))


def transpose_rows(src_ref, dst_ref):
    def block(i, carry):
        at = pl.multiple_of(i * 128, 128)
        dst_ref[0 : src_ref.shape[1], pl.ds(at, 128)] = src_ref[pl.ds(at, 128), :].T
        return carry

    lax.fori_loop(0, ROWS // 128, block, 0)


def window_rows(w):
    return slice(w * TOK, (w + 1) * TOK) if isinstance(w, int) else pl.ds(pl.multiple_of(w * TOK, 16), TOK)


def zero_tail(ref, windows):
    at = windows * TOK
    ref[at:ROWS, :] = jnp.zeros((ROWS - at, ref.shape[1]), ref.dtype)


def half_diag(x, half, mask_ref):
    lanes = slice(half * 128, (half + 1) * 128)
    part = x[0:128, lanes].reshape(8, 16, 128)
    heads = range(half * GHEADS // 2, (half + 1) * GHEADS // 2)
    return jnp.concatenate([(part * mask_ref[h, :, lanes][None]).reshape(128, 128) for h in heads], 0)


def rest_diag(x, mask_ref):
    return jnp.concatenate([x[128:144] * mask_ref[h] for h in range(GHEADS)], 0)


def split_diag(x, mask_ref):
    return half_diag(x, 0, mask_ref), half_diag(x, 1, mask_ref), rest_diag(x, mask_ref)


def against_heads(x, split):
    first, second, rest = split
    return jnp.concatenate([dot_nt(x[:, 0:128], first), dot_nt(x[:, 128:256], second), dot_nt(x, rest)], 1)


def over_queries(m, split):
    first, second, rest = split
    return jnp.concatenate([dot(m[:, 0:512], first), dot(m[:, 512:1024], second)], 1) + dot(m[:, 1024:], rest)


def attention_forward(windows, x_ref, small_ref, line_ref, mask_ref, wq_ref, wp_ref,
                      qkv_ref, pt_ref, o_ref, x1_ref, n1t_ref, vec_ref, n1_ref, bias_ref, tmp_ref):
    tab = unpack_small(small_ref, vec_ref)
    spread_table(tab, line_ref, tmp_ref)
    place_bias(tmp_ref, bias_ref)
    zero_tail(n1_ref, windows)
    zero_tail(o_ref, windows)

    def first_norm(w, carry):
        xhat, _ = norm_parts(x_ref[window_rows(w), :].astype(full))
        n1_ref[window_rows(w), :] = (xhat * vec_ref[0:1, :] + vec_ref[1:2, :]).astype(low)
        return carry

    lax.fori_loop(0, windows, first_norm, 0)
    transpose_rows(n1_ref, n1t_ref)

    def group(g, carry):
        cols = pl.ds(pl.multiple_of(g * GCOLS, GCOLS), GCOLS)
        n1 = n1_ref[...]
        qkv_ref[g] = ((dot(n1, flat(wq_ref[g, 0])) + vec_ref[2:3, cols]) * (HEAD_DIM**-0.5)).astype(low)
        qkv_ref[GROUPS + g] = dot(n1, flat(wq_ref[g, 1])).astype(low)
        qkv_ref[2 * GROUPS + g] = (dot(n1, flat(wq_ref[g, 2])) + vec_ref[3:4, cols]).astype(low)

        def window(w, inner):
            rows = window_rows(w)
            q = qkv_ref[g, rows, :]
            k = qkv_ref[GROUPS + g, rows, :]
            v = qkv_ref[2 * GROUPS + g, rows, :]
            s = dot_nt(k, diag(q, mask_ref)) + bias_ref[g]
            e = jnp.exp(s - jnp.max(s, 0, keepdims=True))
            p = (e * (1.0 / jnp.sum(e, 0, keepdims=True))).astype(low)
            pt_ref[g, w] = p
            o_ref[rows, cols] = undiag(v.T, p, mask_ref).astype(low)
            return inner

        lax.fori_loop(0, windows, window, 0)
        return carry

    lax.fori_loop(0, GROUPS, group, 0)

    def output(w, carry):
        rows = window_rows(w)
        branch = dot(o_ref[rows, :], flat(wp_ref[...])) + vec_ref[4:5, :]
        x1_ref[rows, :] = x_ref[rows, :].astype(full) + branch
        return carry

    lax.fori_loop(0, windows, output, 0)


def gelu_both(h):
    c = math.sqrt(2.0 / math.pi)
    square = h * h
    t = jnp.tanh(h * (c + (c * 0.044715) * square))
    half = 0.5 + 0.5 * t
    act = h * half
    return act, half + act * (1.0 - half) * (2.0 * c + (6.0 * c * 0.044715) * square)


def feed_forward(windows, x1_ref, dy_ref, live_ref, vec_ref, up_ref, down_ref, wp_ref, o_ref,
                 out_ref, dx1_ref, do_ref, gup_ref, gdown_ref, gout_ref, sums_ref,
                 n2_ref, n2t_ref, dy2_ref, dyt_ref, y_ref, dn_ref, bu_ref, bsum_ref):
    zero_tail(n2_ref, windows)
    zero_tail(dy2_ref, windows)

    def second_norm(w, carry):
        rows = window_rows(w)
        xhat, _ = norm_parts(x1_ref[rows, :])
        n2_ref[rows, :] = (xhat * vec_ref[5:6, :] + vec_ref[6:7, :]).astype(low)
        dy2_ref[rows, :] = (dy_ref[rows, :].astype(full) * live_ref[w]).astype(low)
        return carry

    lax.fori_loop(0, windows, second_norm, 0)
    transpose_rows(n2_ref, n2t_ref)
    transpose_rows(dy2_ref, dyt_ref)
    y_ref[...] = jnp.zeros_like(y_ref)
    dn_ref[...] = jnp.zeros_like(dn_ref)
    owners = gup_ref.shape[1]
    for t in range(TILES):
        for s in range(TILE // 128):
            row, at = hidden_place(t, s)
            bu_ref[t, :, s * 128 : (s + 1) * 128] = vec_ref[row : row + 1, at : at + 128]

    def step(t, carry):
        for part in range(TILE // SUB):
            cols = slice(part * SUB, (part + 1) * SUB)
            up = flat(up_ref[t, :, :, cols])
            down = flat(down_ref[t, part * SUB // 128 : (part + 1) * SUB // 128])
            h = dot(n2_ref[...], up) + bu_ref[t, :, cols]
            da = dot_nt(dy2_ref[...], down)
            act, slope = gelu_both(h)
            a = act.astype(low)
            dh = (da * slope).astype(low)
            bsum_ref[t, :, cols] = jnp.sum(dh.astype(full), 0, keepdims=True)
            y_ref[...] += dot(a, down)
            dn_ref[...] += dot_nt(dh, up)
            gd = dot(dyt_ref[...], a).astype(low)
            for b in range(SUB // 128):
                gdown_ref[t, part * SUB // 128 + b] = gd[:, b * 128 : (b + 1) * 128]
            gup_ref[t, :, :, cols] = blocks(dot(n2t_ref[...], dh).astype(low), owners)
        return carry

    lax.fori_loop(0, TILES, step, 0)
    sums_ref[...] = jnp.zeros_like(sums_ref)
    for t in range(TILES):
        for s in range(TILE // 128):
            row, at = hidden_place(t, s)
            sums_ref[row : row + 1, at : at + 128] = bsum_ref[t, :, s * 128 : (s + 1) * 128]
    zero_tail(dx1_ref, windows)

    def finish(w, carry):
        rows = window_rows(w)
        x1 = x1_ref[rows, :]
        out_ref[rows, :] = ((x1 + y_ref[rows, :] + vec_ref[7:8, :]) * live_ref[w]).astype(low)
        xhat, scale = norm_parts(x1)
        dn = dn_ref[rows, :]
        dy = dy2_ref[rows, :].astype(full)
        dx1 = dy + norm_back(xhat, scale, dn, vec_ref[5:6, :])
        dx1_ref[rows, :] = dx1
        dr = dx1.astype(low)
        n2_ref[rows, :] = dr
        do_ref[rows, :] = dot_nt(dr, flat(wp_ref[...])).astype(low)
        sums_ref[4:5, :] += jnp.sum(dr.astype(full), 0, keepdims=True)
        sums_ref[5:6, :] += jnp.sum(dn * xhat, 0, keepdims=True)
        sums_ref[6:7, :] += jnp.sum(dn, 0, keepdims=True)
        sums_ref[7:8, :] += jnp.sum(dy, 0, keepdims=True)
        return carry

    lax.fori_loop(0, windows, finish, 0)
    transpose_rows(o_ref, dyt_ref)
    for g in range(GROUPS):
        at = pl.ds(g * GCOLS, GCOLS)
        gout_ref[:, :, at] = blocks(dot(dyt_ref[...], n2_ref[:, at]).astype(low), gout_ref.shape[0])


def attention_backward(windows, x_ref, vec_ref, line_ref, mask_ref, wq_ref, qkv_ref, pt_ref, do_ref, dx1_ref, n1t_ref, sums_in_ref,
                       gq_ref, gsmall_ref, grad_ref, sums_ref, bias_ref, tmp_ref, dproj_ref, dn_ref):
    bias_ref[...] = jnp.zeros_like(bias_ref)
    dn_ref[...] = jnp.zeros_like(dn_ref)
    sums_ref[...] = sums_in_ref[...]
    for part in range(3):
        dproj_ref[part, windows * TOK :, :] = jnp.zeros((ROWS - windows * TOK, GCOLS), low)

    def group(g, carry):
        cols = pl.ds(pl.multiple_of(g * GCOLS, GCOLS), GCOLS)

        def window(w, inner):
            rows = window_rows(w)
            q = qkv_ref[g, rows, :]
            k = qkv_ref[GROUPS + g, rows, :]
            v = qkv_ref[2 * GROUPS + g, rows, :]
            p = pt_ref[g, w]
            do = diag(do_ref[rows, cols], mask_ref)
            dp = dot_nt(v, do)
            dv = dot(p, do)
            pf = p.astype(full)
            ds = (pf * (dp - jnp.sum(pf * dp, 0, keepdims=True))).astype(low)
            bias_ref[g] += ds.astype(full)
            dk = dot(ds, diag(q, mask_ref))
            dq = undiag(k.T, ds, mask_ref) * (HEAD_DIM**-0.5)
            dq = dq.astype(low)
            dv = dv.astype(low)
            dproj_ref[0, rows, :] = dq
            dproj_ref[1, rows, :] = dk.astype(low)
            dproj_ref[2, rows, :] = dv
            sums_ref[2:3, cols] += jnp.sum(dq.astype(full), 0, keepdims=True)
            sums_ref[3:4, cols] += jnp.sum(dv.astype(full), 0, keepdims=True)
            return inner

        lax.fori_loop(0, windows, window, 0)
        for part in range(3):
            d = dproj_ref[part]
            gq_ref[g, part] = blocks(dot(n1t_ref[...], d).astype(low), gq_ref.shape[2])
            dn_ref[...] += dot_nt(d, flat(wq_ref[g, part]))
        return carry

    lax.fori_loop(0, GROUPS, group, 0)

    def finish(w, carry):
        rows = window_rows(w)
        xhat, scale = norm_parts(x_ref[rows, :].astype(full))
        dn = dn_ref[rows, :]
        grad_ref[rows, :] = dx1_ref[rows, :] + norm_back(xhat, scale, dn, vec_ref[0:1, :])
        sums_ref[0:1, :] += jnp.sum(dn * xhat, 0, keepdims=True)
        sums_ref[1:2, :] += jnp.sum(dn, 0, keepdims=True)
        return carry

    lax.fori_loop(0, windows, finish, 0)
    pack_small(sums_ref[...], table_grad(line_ref, tmp_ref, bias_ref), gsmall_ref)


MESH = pl.DeviceIdType.MESH
REPS = 4
OWNERS = 8
LINKS = OWNERS // 2


class Spot:
    def __init__(self):
        self.rep = lax.axis_index("rep")
        self.shard = lax.axis_index("shard")
        self.z = self.shard // 2
        self.core = self.shard % 2

    def sibling(self):
        return (self.rep, self.z * 2 + (1 - self.core))

    def along_z(self, step):
        return (self.rep, ((self.z + step) % LINKS) * 2 + self.core)

    def turned(self, axis):
        x, y = self.rep % 2, self.rep // 2
        return y * 2 + (1 - x) if axis == 0 else (1 - y) * 2 + x

    def beside(self, axis):
        return (self.turned(axis), self.shard)

    def across(self):
        return (REPS - 1 - self.rep, self.shard)


def greet(spot):
    barrier = pltpu.get_barrier_semaphore()
    peers = [(spot.rep, (spot.shard + i) % OWNERS) for i in range(1, OWNERS)]
    peers += [((spot.rep + i) % REPS, spot.shard) for i in range(1, REPS)]
    for peer in peers:
        pl.semaphore_signal(barrier, inc=1, device_id=peer, device_id_type=MESH)
    return barrier, len(peers)


def send(src, dst, send_sem, recv_sem, peer):
    pltpu.make_async_remote_copy(src_ref=src, dst_ref=dst, send_sem=send_sem, recv_sem=recv_sem, device_id=peer, device_id_type=MESH).start()


def await_bytes(ref, sem):
    pltpu.make_async_copy(ref, ref, sem).wait()


def quarter(ref, rep):
    rows, cols = ref.shape[-2:]
    lead = (slice(None),) * (len(ref.shape) - 2)
    top = pl.multiple_of((rep // 2) * (rows // 2), 16)
    left = pl.multiple_of((rep % 2) * (cols // 2), 128)
    return ref.at[lead + (pl.ds(top, rows // 2), pl.ds(left, cols // 2))]


def half(ref, rep, axis):
    rows, cols = ref.shape[-2:]
    lead = (slice(None),) * (len(ref.shape) - 2)
    if axis == 0:
        left = pl.multiple_of((rep % 2) * (cols // 2), 128)
        return ref.at[lead + (slice(None), pl.ds(left, cols // 2))]
    top = pl.multiple_of((rep // 2) * (rows // 2), 16)
    return ref.at[lead + (pl.ds(top, rows // 2), slice(None))]


class Gather:
    KINDS = (LINKS - 1, LINKS - 1, LINKS - 1, LINKS - 1, LINKS)
    SEMS = 2 * sum(KINDS)
    STAGES = ("start", "across", "relay", "beside", "finish")

    def __init__(self, spot, place, axis, sems, direct=False):
        self.spot, self.place, self.axis, self.sems, self.direct = spot, place, axis, sems, direct

    def sem(self, side, kind, i):
        return self.sems.at[side * (self.SEMS // 2) + sum(self.KINDS[:kind]) + i]

    def block(self, step):
        return self.place(((self.spot.z - step + LINKS) % LINKS) * 2 + self.spot.core)

    def other(self, step):
        return self.place(((self.spot.z - step + LINKS) % LINKS) * 2 + 1 - self.spot.core)

    def start(self):
        spot = self.spot
        mine = self.block(0)
        for i in range(1, LINKS):
            piece = quarter(mine, spot.rep)
            send(piece, piece, self.sem(0, 0, i - 1), self.sem(1, 0, i - 1), spot.along_z(i))
        send(mine, mine, self.sem(0, 4, 0), self.sem(1, 4, 0), spot.sibling())

    def across(self):
        spot = self.spot
        for i in range(1, LINKS):
            piece = quarter(self.block(i), spot.rep)
            await_bytes(piece, self.sem(1, 0, i - 1))
            for axis in (self.axis, 1 - self.axis):
                send(piece, piece, self.sem(0, 1 + axis, i - 1), self.sem(1, 1 + axis, i - 1), spot.beside(axis))
            if self.direct:
                send(piece, piece, self.sem(0, 3, i - 1), self.sem(1, 3, i - 1), spot.across())

    def relay(self):
        spot = self.spot
        if self.direct:
            return
        for i in range(1, LINKS):
            piece = quarter(self.block(i), spot.turned(self.axis))
            await_bytes(piece, self.sem(1, 1 + self.axis, i - 1))
            send(piece, piece, self.sem(0, 3, i - 1), self.sem(1, 3, i - 1), spot.beside(1 - self.axis))

    def beside(self):
        spot = self.spot
        for i in range(1, LINKS):
            block = self.block(i)
            piece = quarter(block, spot.rep)
            if self.direct:
                await_bytes(piece, self.sem(1, 1 + self.axis, i - 1))
            await_bytes(piece, self.sem(1, 2 - self.axis, i - 1))
            await_bytes(piece, self.sem(1, 3, i - 1))
            send(block, block, self.sem(0, 4, i), self.sem(1, 4, i), spot.sibling())

    def finish(self):
        for i in range(LINKS):
            await_bytes(self.other(i), self.sem(1, 4, i))

    def close(self):
        piece = quarter(self.block(0), self.spot.rep)
        for kind in range(4):
            for i in range(1, LINKS):
                await_bytes(piece, self.sem(0, kind, i - 1))
        for i in range(LINKS):
            await_bytes(self.block(i), self.sem(0, 4, i))


class Reduce:
    KINDS = (LINKS, 1, 1, LINKS - 1, REPS - 1)
    SEMS = 2 * sum(KINDS)
    STAGES = ("start", "first", "second", "along", "spread", "passed", "finish")

    def __init__(self, spot, place, out, core_sum, halves, quarters, links, axis, sems, direct):
        self.spot, self.place, self.out, self.axis, self.sems, self.direct = spot, place, out, axis, sems, direct
        self.core_sum, self.halves, self.quarters, self.links = core_sum, halves, quarters, links

    def sem(self, side, kind, i):
        return self.sems.at[side * (self.SEMS // 2) + sum(self.KINDS[:kind]) + i]

    def start(self):
        spot = self.spot
        for z in range(LINKS):
            send(self.place(z * 2 + (1 - spot.core)), self.core_sum.at[z], self.sem(0, 0, z), self.sem(1, 0, z), spot.sibling())

    def first(self):
        spot = self.spot
        for z in range(LINKS):
            total = self.core_sum.at[z]
            await_bytes(total, self.sem(1, 0, z))
            total[...] = (total[...].astype(full) + self.place(z * 2 + spot.core)[...].astype(full)).astype(low)
        theirs = half(self.core_sum, spot.turned(self.axis), self.axis)
        send(theirs, self.halves, self.sem(0, 1, 0), self.sem(1, 1, 0), spot.beside(self.axis))

    def second(self):
        spot = self.spot
        await_bytes(self.halves, self.sem(1, 1, 0))
        mine = half(self.core_sum, spot.rep, self.axis)
        self.halves[...] = (self.halves[...].astype(full) + mine[...].astype(full)).astype(low)
        theirs = half(self.halves, spot.turned(1 - self.axis), 1 - self.axis)
        send(theirs, self.quarters, self.sem(0, 2, 0), self.sem(1, 2, 0), spot.beside(1 - self.axis))

    def along(self):
        spot = self.spot
        await_bytes(self.quarters, self.sem(1, 2, 0))
        mine = half(self.halves, spot.rep, 1 - self.axis)
        self.quarters[...] = (self.quarters[...].astype(full) + mine[...].astype(full)).astype(low)
        for i in range(1, LINKS):
            send(self.quarters.at[(spot.z + i) % LINKS], self.links.at[i - 1], self.sem(0, 3, i - 1), self.sem(1, 3, i - 1), spot.along_z(i))

    def spread(self):
        spot = self.spot
        total = self.quarters[spot.z].astype(full)
        for i in range(1, LINKS):
            await_bytes(self.links.at[i - 1], self.sem(1, 3, i - 1))
            total = total + self.links[i - 1].astype(full)
        mine = quarter(self.out, spot.rep)
        mine[...] = total.astype(low)
        for axis in (self.axis, 1 - self.axis):
            send(mine, mine, self.sem(0, 4, axis), self.sem(1, 4, axis), spot.beside(axis))
        if self.direct:
            send(mine, mine, self.sem(0, 4, 2), self.sem(1, 4, 2), spot.across())

    def passed(self):
        spot = self.spot
        theirs = quarter(self.out, spot.turned(self.axis))
        await_bytes(theirs, self.sem(1, 4, self.axis))
        if not self.direct:
            send(theirs, theirs, self.sem(0, 4, 2), self.sem(1, 4, 2), spot.beside(1 - self.axis))

    def finish(self):
        spot = self.spot
        await_bytes(quarter(self.out, spot.turned(1 - self.axis)), self.sem(1, 4, 1 - self.axis))
        await_bytes(quarter(self.out, REPS - 1 - spot.rep), self.sem(1, 4, 2))

    def close(self):
        for z in range(LINKS):
            await_bytes(self.core_sum.at[z], self.sem(0, 0, z))
        await_bytes(self.halves, self.sem(0, 1, 0))
        await_bytes(self.quarters, self.sem(0, 2, 0))
        for i in range(1, LINKS):
            await_bytes(self.links.at[i - 1], self.sem(0, 3, i - 1))
        for j in range(1, REPS):
            await_bytes(quarter(self.out, self.spot.rep), self.sem(0, 4, j - 1))


class ReduceDirect(Reduce):
    KINDS = (LINKS, REPS - 1, 0, LINKS - 1, REPS - 1)
    SEMS = 2 * sum(KINDS)

    def peers(self):
        spot = self.spot
        return (spot.turned(0), spot.turned(1), REPS - 1 - spot.rep)

    def first(self):
        spot = self.spot
        for z in range(LINKS):
            total = self.core_sum.at[z]
            await_bytes(total, self.sem(1, 0, z))
            total[...] = (total[...].astype(full) + self.place(z * 2 + spot.core)[...].astype(full)).astype(low)
        for j, rep in enumerate(self.peers()):
            send(quarter(self.core_sum, rep), self.halves.at[j], self.sem(0, 1, j), self.sem(1, 1, j), (rep, spot.shard))

    def second(self):
        pass

    def along(self):
        spot = self.spot
        total = quarter(self.core_sum, spot.rep)[...].astype(full)
        for j in range(REPS - 1):
            await_bytes(self.halves.at[j], self.sem(1, 1, j))
            total = total + self.halves[j].astype(full)
        self.quarters[...] = total.astype(low)
        for i in range(1, LINKS):
            send(self.quarters.at[(spot.z + i) % LINKS], self.links.at[i - 1], self.sem(0, 3, i - 1), self.sem(1, 3, i - 1), spot.along_z(i))

    def close(self):
        for z in range(LINKS):
            await_bytes(self.core_sum.at[z], self.sem(0, 0, z))
        for j in range(REPS - 1):
            await_bytes(self.halves.at[j], self.sem(0, 1, j))
        for i in range(1, LINKS):
            await_bytes(self.links.at[i - 1], self.sem(0, 3, i - 1))
        for j in range(1, REPS):
            await_bytes(quarter(self.out, self.spot.rep), self.sem(0, 4, j - 1))


class ReduceSmall:
    KINDS = (LINKS, LINKS - 1, REPS - 1)
    SEMS = 2 * sum(KINDS)
    STAGES = ("start", "first", "second", "along")

    def __init__(self, spot, terms, out, core_sum, links, parts, sems):
        self.spot, self.terms, self.out, self.core_sum, self.links, self.parts, self.sems = spot, terms, out, core_sum, links, parts, sems

    sem = Reduce.sem

    def start(self):
        spot = self.spot
        for z in range(LINKS):
            send(self.terms.at[z * 2 + (1 - spot.core)], self.core_sum.at[z], self.sem(0, 0, z), self.sem(1, 0, z), spot.sibling())

    def first(self):
        spot = self.spot
        for z in range(LINKS):
            await_bytes(self.core_sum.at[z], self.sem(1, 0, z))
            self.core_sum[z] = self.core_sum[z] + self.terms[z * 2 + spot.core]
        for i in range(1, LINKS):
            send(self.core_sum.at[(spot.z + i) % LINKS], self.links.at[i - 1], self.sem(0, 1, i - 1), self.sem(1, 1, i - 1), spot.along_z(i))

    def second(self):
        spot = self.spot
        total = self.core_sum[spot.z]
        for i in range(1, LINKS):
            await_bytes(self.links.at[i - 1], self.sem(1, 1, i - 1))
            total = total + self.links[i - 1]
        self.parts[spot.rep] = total
        mine = self.parts.at[spot.rep]
        for j in range(1, REPS):
            send(mine, mine, self.sem(0, 2, j - 1), self.sem(1, 2, j - 1), ((spot.rep + j) % REPS, spot.shard))

    def along(self):
        for j in range(1, REPS):
            await_bytes(self.parts.at[(self.spot.rep - j + REPS) % REPS], self.sem(1, 2, j - 1))
        total = self.parts[0]
        for j in range(1, REPS):
            total = total + self.parts[j]
        self.out[...] = total

    def close(self):
        for z in range(LINKS):
            await_bytes(self.core_sum.at[z], self.sem(0, 0, z))
        for i in range(1, LINKS):
            await_bytes(self.links.at[i - 1], self.sem(0, 1, i - 1))
        for j in range(1, REPS):
            await_bytes(self.parts.at[self.spot.rep], self.sem(0, 2, j - 1))


OWNED = C // OWNERS
SLOTS = TILES + 1
GATHERS = 2 * TILES + 1 + GROUPS
REDUCES = 2 * TILES + 1 + (GROUPS - 1) + 3
W_Q0, W_Q1, W_Q2, W_P, W_U0, W_D0, W_U1, W_D1, W_U2, W_D2 = W_ALL = range(10)
G_D0, G_U0, G_D1, G_U1, G_D2, G_U2, G_P, G_Q0, G_Q1, G_Q2, G_K2, G_V2, G_S = G_ALL = range(10, 23)
W_Q, W_U, W_D = (W_Q0, W_Q1, W_Q2), (W_U0, W_U1, W_U2), (W_D0, W_D1, W_D2)
G_D, G_U, G_Q, G_LAST = (G_D0, G_D1, G_D2), (G_U0, G_U1, G_U2), (G_Q0, G_Q1), (G_Q2, G_K2, G_V2)
G_TWO = ()
START, ACROSS, RELAY, BESIDE, ARRIVED = range(5)
FIRST, SECOND, ALONG, SPREAD, PASSED, SUMMED = range(1, 7)
BEFORE = {
    2: ((W_Q0, ACROSS), (W_P, START),),
    3: ((W_Q0, RELAY), (W_Q2, START), (W_U0, START),),
    5: ((W_Q0, BESIDE), (W_Q1, ACROSS),),
}
FORWARD = {
    0: ((W_Q1, RELAY), (W_Q2, ACROSS), (W_P, ACROSS), (W_D0, START), (W_U1, START),),
    4: ((W_Q1, BESIDE), (W_U0, ACROSS),),
    6: ((W_Q2, RELAY), (W_P, RELAY),),
    8: ((W_D0, ACROSS), (W_D1, START),),
    9: ((W_D2, START),),
    11: ((W_Q2, BESIDE), (W_U0, RELAY),),
    13: ((W_U1, ACROSS),),
    14: ((W_U2, START),),
    15: ((W_P, BESIDE), (W_D0, RELAY),),
    17: ((W_D1, ACROSS),),
    19: ((W_U0, BESIDE), (W_U1, RELAY),),
}
MIDDLE = {
    0: ((W_D0, BESIDE),),
    1: ((W_D1, RELAY), (W_U2, ACROSS), (W_D2, ACROSS),),
}
TILE_STEP = {
    0: ((W_U1, BESIDE),),
    1: ((W_D1, BESIDE), (W_U2, RELAY), (W_D2, RELAY),),
    2: ((W_U2, BESIDE), (W_D2, BESIDE),),
    3: ((G_D0, FIRST), (G_U0, FIRST),),
    5: ((G_D0, SECOND), (G_U0, SECOND), (G_D1, FIRST), (G_U1, FIRST),),
}
AFTER_TILES = {
    1: ((G_D0, ALONG),),
    2: ((G_D2, FIRST), (G_U2, FIRST),),
}
BACKWARD = {
    1: ((G_D1, SECOND), (G_U1, SECOND),),
    2: ((G_D0, SPREAD), (G_U0, ALONG),),
    4: ((G_P, FIRST),),
    7: ((G_D0, PASSED), (G_D2, SECOND),),
    8: ((G_D1, ALONG), (G_U2, SECOND),),
    9: ((G_U1, ALONG),),
    10: ((G_Q0, FIRST),),
    11: ((G_U0, SPREAD),),
    14: ((G_D2, ALONG), (G_P, SECOND),),
    15: ((G_Q0, SECOND),),
    17: ((G_U0, PASSED), (G_D1, SPREAD), (G_D1, PASSED), (G_U1, SPREAD), (G_U1, PASSED), (G_Q1, FIRST),),
    19: ((G_U2, ALONG),),
    20: ((G_D0, SUMMED), (G_P, ALONG),),
}
LAST_STEPS = {
    0: ((G_Q2, FIRST), (G_K2, FIRST), (G_V2, FIRST),),
    1: ((G_D2, SPREAD), (G_Q2, SECOND),),
    2: ((G_D2, PASSED), (G_P, SPREAD), (G_Q0, ALONG),),
    3: ((G_U1, SUMMED), (G_Q1, SECOND),),
}


def chunk_shapes():
    out = []
    for _ in range(TILES):
        out += [(128, C), (OWNED, TILE)]
    return out + [(OWNED, C)] + [(3, OWNED, GCOLS)] * (GROUPS - 1) + [(OWNED, GCOLS)] * 3


def reduce_scratch():
    out = []
    for i, dims in enumerate(chunk_shapes()):
        *lead, rows, cols = dims
        near = (rows, cols // 2) if i % 2 == 0 else (rows // 2, cols)
        near = (LINKS, *lead, *near) if i < REDUCES - 3 else (REPS - 1, LINKS, *lead, rows // 2, cols // 2)
        out.append(pltpu.VMEM((LINKS, *dims), low))
        out.append(pltpu.VMEM(near, low))
        out.append(pltpu.VMEM((LINKS, *lead, rows // 2, cols // 2), low))
        out.append(pltpu.VMEM((LINKS - 1, *lead, rows // 2, cols // 2), low))
    out += [pltpu.VMEM((LINKS, 40, 128), full), pltpu.VMEM((LINKS - 1, 40, 128), full), pltpu.VMEM((REPS, 40, 128), full)]
    return out


def layer_kernel(windows, x_hbm, dy_hbm, count_ref, q32, p32, u32, d32, vec_in, tab_in, line_ref, mask_ref,
                 out_hbm, grad_hbm, gq_out, gp_out, gu_out, gd_out, gs_out, qkv_hbm, pt_hbm, n1_hbm, *scratch):
    wq, wp, up, down, small, o_ref, x1_ref, vec_ref, sums_ref, terms_ref = scratch[:10]
    gather_sems, reduce_sems, small_sems, small_reduce_sems, local = scratch[-5:]
    reduce_refs = scratch[10:-5]
    spot = Spot()
    rows_all = windows * TOK

    def live(w):
        return (w < count_ref[0]).astype(full)

    mine = spot.shard
    V = pltpu.VMEM

    jobs = {}
    places = [(W_Q[g], lambda s, g=g: wq.at[g, :, s]) for g in range(GROUPS)] + [(W_P, lambda s: wp.at[s])]
    for t in range(TILES):
        places += [(W_U[t], lambda s, t=t: up.at[t, s]), (W_D[t], lambda s, t=t: down.at[t, s])]
    for i, (name, place) in enumerate(places):
        jobs[name] = Gather(spot, place, i % 2, gather_sems.at[i], direct=name == W_Q0)
    places = []
    for t in range(TILES):
        slot = (t + SLOTS - 1) % SLOTS
        places.append((G_D[t], lambda s, slot=slot: down.at[slot, s], gd_out.at[t]))
        places.append((G_U[t], lambda s, slot=slot: up.at[slot, s], gu_out.at[t]))
    places.append((G_P, lambda s: wp.at[s], gp_out))
    for g in range(GROUPS - 1):
        places.append((G_Q[g], lambda s, g=g: wq.at[g, :, s], gq_out.at[g]))
    for part in range(3):
        places.append((G_LAST[part], lambda s, part=part: up.at[TILES - 1, s, :, pl.ds(part * GCOLS, GCOLS)], gq_out.at[GROUPS - 1, part]))
    for i, (name, place, out) in enumerate(places):
        kind = ReduceDirect if name in G_LAST else Reduce
        jobs[name] = kind(spot, place, out, *reduce_refs[4 * i : 4 * i + 4], i % 2, reduce_sems.at[i], name not in G_TWO)
    jobs[G_S] = ReduceSmall(spot, terms_ref, gs_out, *reduce_refs[-3:], small_reduce_sems)

    done = {}

    def run(name, upto):
        for stage in range(done.get(name, 0), upto + 1):
            getattr(jobs[name], jobs[name].STAGES[stage])()
        done[name] = max(done.get(name, 0), upto + 1)

    def hook(table, place):
        for item in table.get(place, ()):
            run(*item)

    def hook_window(table, g, w):
        for at in range(windows):
            place = g * windows + at
            if place in table:

                @pl.when(w == at)
                def _(place=place):
                    hook(table, place)

    barrier, peers = greet(spot)

    def cast(q_v, p_v, u_v, d_v):
        loads = [pltpu.make_async_copy(a, b, local.at[i]) for i, (a, b) in enumerate(((q32, q_v), (p32, p_v), (u32, u_v), (d32, d_v)))]
        for load in loads:
            load.start()
        small[mine] = jnp.zeros((48, 128), low)
        pad = jnp.zeros((16, 128), full)
        vec_ref[:, 0:128] = pad
        vec_ref[0:12, 0:OWNED] = vec_in[...]
        small[mine, 0:16, :] = vec_ref[:, 0:128].astype(low)
        x1_ref[0:32, 0:128] = jnp.zeros((32, 128), full)
        x1_ref[0:HEADS, 0 : tab_in.shape[1]] = tab_in[...]
        small[mine, 16:48, :] = x1_ref[0:32, 0:128].astype(low)
        loads[0].wait()
        for g in range(GROUPS):
            for part in range(3):
                wq[g, part, mine] = q_v[:, part * C + g * GCOLS : part * C + (g + 1) * GCOLS].astype(low)
        pl.semaphore_wait(barrier, peers)
        for i in range(1, OWNERS):
            send(small.at[mine], small.at[mine], small_sems.at[i], small_sems.at[OWNERS + i], (spot.rep, (mine + i) % OWNERS))
        run(W_Q0, START)
        run(W_Q1, START)
        loads[1].wait()
        wp[mine] = p_v[...].astype(low)
        loads[2].wait()
        loads[3].wait()
        for t in range(TILES):
            for s in range(OWNERS):
                src = (MLP // OWNERS) * s + 128 * t
                up[t, mine, :, s * 128 : (s + 1) * 128] = u_v[:, src : src + 128].astype(low)
            down[t, mine] = d_v[t * 128 : (t + 1) * 128, :].astype(low)

    pl.run_scoped(cast, V((OWNED, 3 * C), full), V((OWNED, C), full), V((OWNED, MLP), full), V((TILES * 128, C), full))

    def forward(dy_ref, dyt_ref, x_ref, n1_ref, qkv_ref, pt_ref, bias_ref):
        load = pltpu.make_async_copy(x_hbm, x_ref, local.at[0])
        load.start()
        load_dy = pltpu.make_async_copy(dy_hbm, dy_ref.at[0:rows_all], local.at[2])
        load_dy.start()
        zero_tail(n1_ref, windows)
        zero_tail(dy_ref, windows)
        zero_tail(o_ref, windows)
        for i in range(1, OWNERS):
            await_bytes(small.at[(mine - i + OWNERS) % OWNERS], small_sems.at[OWNERS + i])
        tab = unpack_small(small, vec_ref)
        hook(BEFORE, 0)
        load.wait()
        hook(BEFORE, 1)

        def first_norm(w, carry):
            xhat, _ = norm_parts(x_ref[window_rows(w), :].astype(full))
            n1_ref[window_rows(w), :] = (xhat * vec_ref[0:1, :] + vec_ref[1:2, :]).astype(low)
            return carry

        lax.fori_loop(0, windows, first_norm, 0)
        hook(BEFORE, 2)
        save = pltpu.make_async_copy(n1_ref, n1_hbm, local.at[1])
        save.start()
        hook(BEFORE, 3)
        load_dy.wait()

        def keep_live(w, carry):
            dy_ref[window_rows(w), :] = (dy_ref[window_rows(w), :].astype(full) * live(w)).astype(low)
            return carry

        lax.fori_loop(0, windows, keep_live, 0)
        transpose_rows(dy_ref, dyt_ref)
        hook(BEFORE, 4)

        def bias(tmp_ref):
            spread_table(tab, line_ref, tmp_ref)
            hook(BEFORE, 5)
            place_bias(tmp_ref, bias_ref)

        pl.run_scoped(bias, V((2, TOK * HEADS, 128), full))
        for g in range(GROUPS):
            cols = slice(g * GCOLS, (g + 1) * GCOLS)
            held = qkv_ref.at[g % 2]
            if g >= 2:
                pltpu.make_async_copy(held, qkv_hbm.at[g - 2], local.at[2 + g % 2]).wait()
            run(W_Q[g], ARRIVED)
            n1 = n1_ref[...]
            held[0] = ((dot(n1, flat(wq[g, 0])) + vec_ref[2:3, cols]) * (HEAD_DIM**-0.5)).astype(low)
            held[1] = dot(n1, flat(wq[g, 1])).astype(low)
            held[2] = (dot(n1, flat(wq[g, 2])) + vec_ref[3:4, cols]).astype(low)
            pltpu.make_async_copy(held, qkv_hbm.at[g], local.at[2 + g % 2]).start()

            def window(w, carry, g=g, cols=cols, held=held):
                hook_window(FORWARD, g, w)
                rows = window_rows(w)
                n = g * windows + w
                slot = n % 2
                s = against_heads(held[1, rows, :], split_diag(held[0, rows, :], mask_ref)) + bias_ref[g]
                e = jnp.exp(s - jnp.max(s, 0, keepdims=True))
                p = (e * (1.0 / jnp.sum(e, 0, keepdims=True))).astype(low)
                keep = pltpu.make_async_copy(pt_ref.at[slot], pt_hbm.at[n], local.at[4 + slot])

                @pl.when(n >= 2)
                def _():
                    keep.wait()

                pt_ref[slot] = p
                keep.start()
                o_ref[rows, cols] = undiag(held[2, rows, :].T, p, mask_ref).astype(low)
                return carry

            lax.fori_loop(0, windows, window, 0)

        run(W_P, ARRIVED)

        x1_ref[...] = x_ref[...].astype(full) + (dot(o_ref[0:rows_all], flat(wp[...])) + vec_ref[4:5, :])
        save.wait()
        for g in (GROUPS - 2, GROUPS - 1):
            pltpu.make_async_copy(qkv_ref.at[g % 2], qkv_hbm.at[g], local.at[2 + g % 2]).wait()
        for slot in range(2):
            pltpu.make_async_copy(pt_ref.at[slot], pt_hbm.at[0], local.at[4 + slot]).wait()

    def middle(dy_ref, dyt_ref, n2_ref, n2t_ref, y_ref, dn_ref, bu_ref, bsum_ref):
        zero_tail(n2_ref, windows)
        hook(MIDDLE, 0)

        def second_norm(w, carry):
            rows = window_rows(w)
            xhat, _ = norm_parts(x1_ref[rows, :])
            n2_ref[rows, :] = (xhat * vec_ref[5:6, :] + vec_ref[6:7, :]).astype(low)
            return carry

        lax.fori_loop(0, windows, second_norm, 0)
        transpose_rows(n2_ref, n2t_ref)
        hook(MIDDLE, 1)
        n2t_ref[C:, :] = jnp.ones((16, ROWS), low)
        y_ref[...] = jnp.zeros_like(y_ref)
        dn_ref[...] = jnp.zeros_like(dn_ref)
        for t in range(TILES):
            for s in range(TILE // 128):
                row, left = hidden_place(t, s)
                bu_ref[t, :, s * 128 : (s + 1) * 128] = vec_ref[row : row + 1, left : left + 128]
        hook(MIDDLE, 2)
        run(W_U0, ARRIVED)
        run(W_D0, ARRIVED)
        hook(TILE_STEP, 0)
        halves = TILE // SUB

        def step(i, carry):
            for k in range(1, TILES * halves):

                @pl.when(i == k)
                def _(k=k):
                    if k % halves == 0:
                        t = k // halves
                        for name in (W_U[t], W_D[t]):
                            run(name, ARRIVED)
                        for name in (W_U[t - 1], W_D[t - 1]):
                            jobs[name].close()
                        for name in (G_D[t - 1], G_U[t - 1]):
                            run(name, START)
                    hook(TILE_STEP, k)

            t, part = i // halves, i % halves
            cols = pl.ds(pl.multiple_of(part * SUB, SUB), SUB)
            wide = SUB // 128
            slot = (t + SLOTS - 1) % SLOTS
            u = flat(up[t, :, :, cols])
            d = flat(down[t, pl.ds(part * wide, wide)])
            h = dot(n2_ref[...], u) + bu_ref[t, :, cols]
            da = dot_nt(dy_ref[...], d)
            act, slope = gelu_both(h)
            a = act.astype(low)
            dh = (da * slope).astype(low)
            y_ref[...] += dot(a, d)
            dn_ref[...] += dot_nt(dh, u)
            gd = dot(dyt_ref[...], a).astype(low)
            down[slot, pl.ds(part * wide, wide)] = blocks(gd.T, wide)
            gu = dot(n2t_ref[...], dh)
            up[slot, :, :, cols] = blocks(gu[0:C].astype(low), OWNERS)
            bsum_ref[t, :, cols] = gu[C : C + 1]
            return carry

        lax.fori_loop(0, TILES * halves, step, 0)
        run(G_D[-1], START)
        run(G_U[-1], START)
        hook(AFTER_TILES, 0)
        sums_ref[...] = jnp.zeros_like(sums_ref)
        for t in range(TILES):
            for s in range(TILE // 128):
                row, left = hidden_place(t, s)
                sums_ref[row : row + 1, left : left + 128] = bsum_ref[t, :, s * 128 : (s + 1) * 128]
        transpose_rows(o_ref, dyt_ref)
        hook(AFTER_TILES, 1)

        def finish(w, carry):
            rows = window_rows(w)
            x1 = x1_ref[rows, :]
            xhat, scale = norm_parts(x1)
            dn = dn_ref[rows, :]
            dy = dy_ref[rows, :].astype(full)
            dx1 = dy + norm_back(xhat, scale, dn, vec_ref[5:6, :])
            dr = dx1.astype(low)
            sums_ref[4:5, :] += jnp.sum(dr.astype(full), 0, keepdims=True)
            sums_ref[5:6, :] += jnp.sum(dn * xhat, 0, keepdims=True)
            sums_ref[6:7, :] += jnp.sum(dn, 0, keepdims=True)
            sums_ref[7:8, :] += jnp.sum(dy, 0, keepdims=True)
            dy_ref[rows, :] = ((x1 + y_ref[rows, :] + vec_ref[7:8, :]) * live(w)).astype(low)
            x1_ref[rows, :] = dx1
            n2_ref[rows, :] = dr
            return carry

        lax.fori_loop(0, windows, finish, 0)
        o_ref[...] = dot_nt(n2_ref[...], flat(wp[...])).astype(low)
        save = pltpu.make_async_copy(dy_ref.at[0:rows_all], out_hbm, local.at[0])
        save.start()
        hook(AFTER_TILES, 2)
        jobs[W_P].close()
        for g in range(GROUPS):
            cols = slice(g * GCOLS, (g + 1) * GCOLS)
            wp[:, :, cols] = blocks(dot(dyt_ref[...], n2_ref[:, cols]).astype(low), OWNERS)
        run(G_P, START)
        hook(AFTER_TILES, 3)
        save.wait()

    def both(dy_ref, dyt_ref):
        pl.run_scoped(functools.partial(forward, dy_ref, dyt_ref), V((rows_all, C), low), V((ROWS, C), low),
                      V((2, 3, ROWS, GCOLS), low), V((2, TOK, PACK), low), V((GROUPS, TOK, PACK), full))
        pl.run_scoped(functools.partial(middle, dy_ref, dyt_ref), V((ROWS, C), low), V((C + 16, ROWS), low), V((ROWS, C), full), V((ROWS, C), full),
                      V((TILES, 1, TILE), full), V((TILES, 1, TILE), full))

    pl.run_scoped(both, V((ROWS, C), low), V((C, ROWS), low))

    def backward(x_ref, n1_ref, n1t_ref, qkv_ref, pt_ref, dproj_ref, dn_ref, bias_ref):
        loads = [pltpu.make_async_copy(x_hbm, x_ref, local.at[0]), pltpu.make_async_copy(n1_hbm, n1_ref, local.at[1])]
        fetch = [pltpu.make_async_copy(qkv_hbm.at[g], qkv_ref.at[g % 2], local.at[2 + g % 2]) for g in range(GROUPS)]
        fetch[0].start()
        pltpu.make_async_copy(pt_hbm.at[0], pt_ref.at[0], local.at[4]).start()
        fetch[1].start()
        for load in loads:
            load.start()
        bias_ref[...] = jnp.zeros_like(bias_ref)
        dn_ref[...] = jnp.zeros_like(dn_ref)
        for part in range(3):
            dproj_ref[part, rows_all:, :] = jnp.zeros((ROWS - rows_all, GCOLS), low)
        for g in range(GROUPS):
            cols = slice(g * GCOLS, (g + 1) * GCOLS)
            held = qkv_ref.at[g % 2]
            fetch[g].wait()

            def window(w, carry, g=g, cols=cols, held=held):
                hook_window(BACKWARD, g, w)
                rows = window_rows(w)
                n = g * windows + w
                slot = n % 2

                @pl.when(n + 1 < GROUPS * windows)
                def _():
                    pltpu.make_async_copy(pt_hbm.at[n + 1], pt_ref.at[1 - slot], local.at[5 - slot]).start()

                pltpu.make_async_copy(pt_hbm.at[n], pt_ref.at[slot], local.at[4 + slot]).wait()
                q = held[0, rows, :]
                k = held[1, rows, :]
                v = held[2, rows, :]
                p = pt_ref[slot]
                do = split_diag(o_ref[rows, cols], mask_ref)
                dp = against_heads(v, do)
                dv = over_queries(p, do).astype(low)
                pf = p.astype(full)
                ds = (pf * (dp - jnp.sum(pf * dp, 0, keepdims=True))).astype(low)
                bias_ref[g] += ds.astype(full)
                dproj_ref[1, rows, :] = over_queries(ds, split_diag(q, mask_ref)).astype(low)
                dq = (undiag(k.T, ds, mask_ref) * (HEAD_DIM**-0.5)).astype(low)
                dproj_ref[0, rows, :] = dq
                dproj_ref[2, rows, :] = dv
                sums_ref[2:3, cols] += jnp.sum(dq.astype(full), 0, keepdims=True)
                sums_ref[3:4, cols] += jnp.sum(dv.astype(full), 0, keepdims=True)
                return carry

            lax.fori_loop(0, windows, window, 0)
            if g + 2 < GROUPS:
                fetch[g + 2].start()
            if g == 0:
                for load in loads:
                    load.wait()
                transpose_rows(n1_ref, n1t_ref)
            jobs[W_Q[g]].close()
            if g == GROUPS - 1:
                jobs[W_U[-1]].close()
                for part in range(3):
                    up[TILES - 1, :, :, part * GCOLS : (part + 1) * GCOLS] = blocks(dot(n1t_ref[...], dproj_ref[part]).astype(low), OWNERS)
                    run(G_LAST[part], START)
                hook(LAST_STEPS, 0)
                for part in range(3):
                    dn_ref[...] += dot_nt(dproj_ref[part], flat(wq[g, part]))
            else:
                for part in range(3):
                    d = dproj_ref[part]
                    dn_ref[...] += dot_nt(d, flat(wq[g, part]))
                    wq[g, part] = blocks(dot(n1t_ref[...], d).astype(low), OWNERS)
                run(G_Q[g], START)

        def last_norm(grad_ref):
            def finish(w, carry):
                rows = window_rows(w)
                slot = w % 2
                xhat, scale = norm_parts(x_ref[rows, :].astype(full))
                dn = dn_ref[rows, :]
                save = pltpu.make_async_copy(grad_ref.at[slot], grad_hbm.at[rows], local.at[4 + slot])

                @pl.when(w >= 2)
                def _():
                    save.wait()

                grad_ref[slot] = x1_ref[rows, :] + norm_back(xhat, scale, dn, vec_ref[0:1, :])
                save.start()
                sums_ref[0:1, :] += jnp.sum(dn * xhat, 0, keepdims=True)
                sums_ref[1:2, :] += jnp.sum(dn, 0, keepdims=True)
                return carry

            lax.fori_loop(0, windows, finish, 0)
            hook(LAST_STEPS, 1)
            for slot in range(2):
                pltpu.make_async_copy(grad_ref.at[slot], grad_hbm.at[pl.ds(0, TOK)], local.at[4 + slot]).wait()

        pl.run_scoped(last_norm, V((2, TOK, C), full))
        hook(LAST_STEPS, 2)

        def table(tmp_ref):
            pack_small(sums_ref[...], table_grad(line_ref, tmp_ref, bias_ref), terms_ref)

        pl.run_scoped(table, V((2, TOK * HEADS, 128), full))
        run(G_S, START)
        hook(LAST_STEPS, 3)
        for stage in range(len(Reduce.STAGES)):
            for name in G_ALL:
                if stage < len(jobs[name].STAGES):
                    run(name, stage)

    pl.run_scoped(backward, V((rows_all, C), low), V((ROWS, C), low), V((C, ROWS), low), V((2, 3, ROWS, GCOLS), low), V((2, TOK, PACK), low), V((3, ROWS, GCOLS), low),
                  V((ROWS, C), full), V((GROUPS, TOK, PACK), full))
    jobs[W_D[-1]].close()
    for i in range(1, OWNERS):
        await_bytes(small.at[mine], small_sems.at[i])
    for name in G_ALL:
        jobs[name].close()


def shape(dims, kind):
    return jax.ShapeDtypeStruct(dims, kind)


def adamw(weight, moment, second, gradient, step_rate):
    moment_new = beta_one * moment + (1.0 - beta_one) * gradient
    second_new = beta_two * second + (1.0 - beta_two) * gradient * gradient
    update = moment_new * (1.0 / (1.0 - beta_one**STEP)) / (jnp.sqrt(second_new * (1.0 / (1.0 - beta_two**STEP))) + adam_eps)
    weight_new = weight * (1.0 - step_rate * weight_decay) - step_rate * update
    return (weight_new, moment_new, second_new)


def update_kernel(*refs):
    gq, gp, gu, gd, gs = refs[:5]
    ins = [refs[5 + 3 * i : 8 + 3 * i] for i in range(6)]
    outs = [refs[25 + 4 * i : 29 + 4 * i] for i in range(4)] + [refs[41:44], refs[44:47]]
    for i in range(2):
        refs[47 + i][...] = refs[23 + i][...]

    def piece(which, place, gradient):
        new = adamw(*(ref[place] for ref in ins[which]), gradient, step_rates[which])
        for ref, value in zip(outs[which], new):
            ref[place] = value
        if which < 4:
            outs[which][3][place] = new[0].astype(low)

    every = (slice(None), slice(None))
    piece(0, every, jnp.concatenate([gq[g, part] for part in range(3) for g in range(GROUPS)], 1).astype(full))
    piece(1, every, gp[...].astype(full))
    piece(2, every, jnp.concatenate([gu[t, :, s * 128 : (s + 1) * 128] for s in range(OWNERS) for t in range(TILES)], 1).astype(full))
    piece(3, every, gd[0].astype(full))

    @pl.when(pl.program_id(0) == 0)
    def _():
        piece(4, every, gs[0:12, 0:OWNED])
        piece(5, every, gs[16:40, 0 : ins[5][0].shape[1]])


def update(gq, gp, gu, gd, gs, states, results):
    steps = OWNED // 16

    def rows_of(array):
        tall = array.shape[0] // steps
        return pl.BlockSpec((tall, array.shape[1]), lambda i: (i, 0))

    def whole(array):
        return pl.BlockSpec(array.shape, lambda i: (0, 0))

    per_tile = 128 * TILES // steps
    specs = [
        pl.BlockSpec((GROUPS, 3, 16, GCOLS), lambda i: (0, 0, i, 0)),
        pl.BlockSpec((16, C), lambda i: (i, 0)),
        pl.BlockSpec((TILES, 16, TILE), lambda i: (0, i, 0)),
        pl.BlockSpec((1, per_tile, C), lambda i: (i // (128 // per_tile), i % (128 // per_tile), 0)),
        whole(gs),
    ]
    out_shapes, out_specs = [], []
    for i, group in enumerate(states):
        for array in group:
            specs.append(rows_of(array) if i < 4 else whole(array))
            out_shapes.append(shape(array.shape, full))
            out_specs.append(specs[-1])
        if i < 4:
            out_shapes.append(shape(group[0].shape, low))
            out_specs.append(rows_of(group[0]))
    results = [array.reshape(steps, -1, C) for array in results]
    for array in results:
        specs.append(pl.BlockSpec((1, *array.shape[1:]), lambda i: (i, 0, 0)))
        out_shapes.append(shape(array.shape, array.dtype))
        out_specs.append(specs[-1])
    return pl.pallas_call(
        update_kernel,
        grid=(steps,),
        in_specs=specs,
        out_specs=out_specs,
        out_shape=out_shapes,
        compiler_params=pltpu.CompilerParams(vmem_limit_bytes=63 * MIB),
        name="update",
    )(gq, gp, gu, gd, gs, *[array for group in states for array in group], *results)


def shards(
    tokens, out_grad, window_count,
    qkv_weight, qkv_first, qkv_second,
    output_weight, output_first, output_second,
    up_weight, up_first, up_second,
    down_weight, down_first, down_second,
    vectors, vector_first, vector_second,
    bias_table, table_first, table_second,
):
    windows = tokens.shape[0]
    rows = windows * TOK
    V = pltpu.VMEM
    D = pltpu.SemaphoreType.DMA
    hbm = pl.BlockSpec(memory_space=pl.ANY)
    vmem = pl.BlockSpec(memory_space=pltpu.VMEM)
    result = pl.pallas_call(
        functools.partial(layer_kernel, windows),
        out_shape=[
            shape((rows, C), low), shape((rows, C), full),
            shape((GROUPS, 3, OWNED, GCOLS), low), shape((OWNED, C), low), shape((TILES, OWNED, TILE), low), shape((TILES, 128, C), low),
            shape((40, 128), full),
            shape((GROUPS, 3, ROWS, GCOLS), low), shape((GROUPS * windows, TOK, PACK), low), shape((ROWS, C), low)],
        in_specs=[hbm, hbm, pl.BlockSpec(memory_space=pltpu.SMEM)] + [hbm] * 4 + [vmem] * 4,
        out_specs=[hbm, hbm] + [vmem] * 5 + [hbm] * 3,
        scratch_shapes=[
            V((GROUPS, 3, OWNERS, OWNED, GCOLS), low), V((OWNERS, OWNED, C), low), V((SLOTS, OWNERS, OWNED, TILE), low),
            V((SLOTS, OWNERS, 128, C), low), V((OWNERS, 48, 128), low), V((ROWS, C), low), V((rows, C), full), V((16, C), full), V((16, C), full),
            V((OWNERS, 40, 128), full)]
        + reduce_scratch()
        + [D((GATHERS, Gather.SEMS)), D((REDUCES, ReduceDirect.SEMS)), D((2 * OWNERS,)), D((ReduceSmall.SEMS,)), D((6,))],
        compiler_params=pltpu.CompilerParams(vmem_limit_bytes=63 * MIB, collective_id=0, has_side_effects=True),
        name="layer",
    )(tokens.reshape(rows, C), out_grad.reshape(rows, C), window_count, qkv_weight, output_weight, up_weight, down_weight, vectors, bias_table.T,
      jnp.asarray(line_matrix(), low), jnp.asarray(head_masks(), low))
    out, grad, gq, gp, gu, gd, gs = result[:7]
    new = update(gq, gp, gu, gd, gs, (
        (qkv_weight, qkv_first, qkv_second), (output_weight, output_first, output_second), (up_weight, up_first, up_second),
        (down_weight, down_first, down_second), (vectors, vector_first, vector_second), (bias_table.T, table_first.T, table_second.T)), (out, grad))
    *new, out, grad = new
    return (out.reshape(tokens.shape), grad.reshape(tokens.shape), *new[:-3], *(array.T for array in new[-3:]))


def vmem_call(body, outs, scratch, args, name, limit=60, **params):
    spec = pl.BlockSpec(memory_space=pltpu.VMEM)
    return pl.pallas_call(
        body,
        out_shape=outs,
        in_specs=[pl.BlockSpec(memory_space=pltpu.SMEM) if a.dtype == full and a.ndim == 1 else spec for a in args],
        out_specs=[spec] * len(outs),
        scratch_shapes=scratch,
        compiler_params=pltpu.CompilerParams(vmem_limit_bytes=limit * MIB, **params),
        name=name,
    )(*args)


def local_step(tokens, out_grad, window_count, small, wq, wp, up, down):
    windows = tokens.shape[0]
    rows = windows * TOK
    owned = C // OWNERS
    V = pltpu.VMEM
    x = tokens.reshape(rows, C)
    dy = out_grad.reshape(rows, C)
    live = (jnp.arange(windows) < window_count[0]).astype(full)
    line = jnp.asarray(line_matrix(), low)
    masks = jnp.asarray(head_masks(), low)
    qkv, pt, o, x1, n1t, vec = vmem_call(
        functools.partial(attention_forward, windows),
        [shape((9, ROWS, GCOLS), low), shape((GROUPS, windows, TOK, PACK), low), shape((ROWS, C), low), shape((rows, C), full), shape((C, ROWS), low),
         shape((16, C), full)],
        [V((ROWS, C), low), V((GROUPS, TOK, PACK), full), V((2, TOK * HEADS, 128), full)],
        (x, small, line, masks, wq, wp), "attention_forward")
    out, dx1, do, gup, gdown, gout, sums = vmem_call(
        functools.partial(feed_forward, windows),
        [shape((rows, C), low), shape((ROWS, C), full), shape((rows, C), low), shape((TILES, OWNERS, owned, TILE), low),
         shape((TILES, OWNERS, C, 128), low), shape((OWNERS, owned, C), low), shape((16, C), full)],
        [V((ROWS, C), low), V((C, ROWS), low), V((ROWS, C), low), V((C, ROWS), low), V((ROWS, C), full), V((ROWS, C), full),
         V((TILES, 1, TILE), full), V((TILES, 1, TILE), full)],
        (x1, dy, live, vec, up, down, wp, o), "feed_forward")
    gq, gsmall, grad = vmem_call(
        functools.partial(attention_backward, windows),
        [shape((GROUPS, 3, OWNERS, owned, GCOLS), low), shape((OWNERS, 40, 128), full), shape((rows, C), full)],
        [V((16, C), full), V((GROUPS, TOK, PACK), full), V((2, TOK * HEADS, 128), full), V((3, ROWS, GCOLS), low), V((ROWS, C), full)],
        (x, vec, line, masks, wq, qkv, pt, do, dx1, n1t, sums), "attention_backward")
    return out.reshape(tokens.shape), grad.reshape(tokens.shape), gq, gout, gup, gdown, gsmall


def shards_general(
    tokens, out_grad, window_count,
    qkv_weight, qkv_first, qkv_second,
    output_weight, output_first, output_second,
    up_weight, up_first, up_second,
    down_weight, down_first, down_second,
    vectors, vector_first, vector_second,
    bias_table, table_first, table_second,
):
    gather = functools.partial(lax.all_gather, axis_name="shard", tiled=True)
    scatter = functools.partial(lax.psum_scatter, axis_name="shard", tiled=True)
    owned = C // OWNERS
    wq = gather(qkv_weight.astype(low), axis=0).reshape(OWNERS, owned, 3, GROUPS, GCOLS).transpose(3, 2, 0, 1, 4)
    wp = gather(output_weight.astype(low), axis=0).reshape(OWNERS, owned, C)
    up = gather(up_weight.astype(low), axis=0).reshape(OWNERS, owned, OWNERS, TILES, 128).transpose(3, 0, 1, 2, 4)
    up = up.reshape(TILES, OWNERS, owned, TILE)
    down = gather(down_weight.astype(low), axis=0).reshape(OWNERS, TILES, 128, C).transpose(1, 0, 2, 3)
    vec = gather(vectors.astype(low), axis=1)
    tab = gather(bias_table.astype(low), axis=0)
    table_rows = tab.shape[0]
    count = TAB_ROWS // OWNERS
    vec = vec.reshape(12, OWNERS, owned).transpose(1, 0, 2)
    tab = tab[:TAB_ROWS].reshape(OWNERS, count, HEADS).transpose(0, 2, 1)
    small = jnp.concatenate([jnp.pad(vec, ((0, 0), (0, 4), (0, 128 - owned))), jnp.pad(tab, ((0, 0), (0, 8), (0, 128 - count)))], 1)
    out, grad, gq, gp, gu, gd, gs = local_step(tokens, out_grad, window_count, small, wq, wp, up, down)
    gq = gq.astype(full).transpose(2, 3, 1, 0, 4).reshape(C, 3 * C)
    gu = gu.astype(full).reshape(TILES, C, OWNERS, 128).transpose(1, 2, 0, 3).reshape(C, MLP)
    gd = gd.astype(full).transpose(1, 0, 3, 2).reshape(MLP, C)
    gv = gs[:, :12, :owned].transpose(1, 0, 2).reshape(12, C)
    gb = gs[:, 16:40, :count].transpose(0, 2, 1).reshape(TAB_ROWS, HEADS)
    gb = jnp.pad(gb, ((0, table_rows - TAB_ROWS), (0, 0)))
    totals = lax.psum(
        (scatter(gq, scatter_dimension=0), scatter(gp.astype(full).reshape(C, C), scatter_dimension=0), scatter(gu, scatter_dimension=0),
         scatter(gd, scatter_dimension=0), scatter(gv, scatter_dimension=1), scatter(gb, scatter_dimension=0)), "rep")
    states = (
        (qkv_weight, qkv_first, qkv_second), (output_weight, output_first, output_second), (up_weight, up_first, up_second),
        (down_weight, down_first, down_second), (vectors, vector_first, vector_second), (bias_table, table_first, table_second))
    results = [out, grad]
    for i, (state, total, rate) in enumerate(zip(states, totals, step_rates)):
        new = adamw(*state, total, rate)
        results += [*new, new[0].astype(low)] if i < 4 else [*new]
    return tuple(results)


def solution(mesh):
    wins = P(("rep", "shard"), None, None)
    rows = P("shard", None)
    cols = P(None, "shard")
    fits = mesh.shape["rep"] == REPS and mesh.shape["shard"] == OWNERS
    return jax.shard_map(
        shards if fits else shards_general,
        mesh=mesh,
        in_specs=(wins, wins, P(("rep", "shard"))) + (rows,) * 12 + (cols,) * 3 + (rows,) * 3,
        out_specs=(wins, wins) + (rows,) * 16 + (cols,) * 3 + (rows,) * 3,
        check_vma=False,
    )
```

profile of v0, /device:TPU:0, one launch (start us, length us, event | category | flops | bytes accessed | tf_op | source)
XLA Modules:
  0.0 197.5 jit_solution(6832865705489546345)
XLA Ops:
  1.3 182.2 %layer.1 = (bf16[1008,768]{1,0:T(8,128)(2,1)}, f32[1008,768]{1,0:T(8,128)}, bf16[3,3,96,256]{3,2,1,0:T(8,128)(2,1)}, bf16[96,768]{1,0:T(8,128)(2,1)}, bf16[3,96,...) custom-call(bf16[1008,768]{1,0:T(8,128)(2,1)} %bitcast.13, ...), custom_call_target="tpu_custom_call" | custom-call | tf_op jit(solution)/shard_map/layer/pallas_call | solution.py:1318
  183.5 13.8 %update.1 = (f32[96,2304]{1,0:T(8,128)}, f32[96,2304]{1,0:T(8,128)}, f32[96,2304]{1,0:T(8,128)}, bf16[96,2304]{1,0:T(8,128)(2,1)}, f32[96,768]{1,0:T(8,128)}, /*...) custom-call(bf16[3,3,96,256]{3,2,1,0:T(8,128)(2,1)} %get-tuple-eleme, ...), custom_call_target="tpu_custom_call" | custom-call | tf_op jit(solution)/shard_map/update/pallas_call | solution.py:1292
where the time goes:
time: 198 us
  Pallas kernels  196 us (99%)
    pallas_call x1, Pallas kernels, shards(): pl.pallas_call(functools.partial(layer_kernel, windows), out_shape=[shape...  182 us
    pallas_call x1, Pallas kernels, update(): pl.pallas_call(update_kernel, grid=(steps,), in_specs=specs, out_specs=ou...  13.8 us

commit v1 on v0

--- a/solution.py
+++ b/solution.py
@@ -744,58 +744,59 @@
 START, ACROSS, RELAY, BESIDE, ARRIVED = range(5)
 FIRST, SECOND, ALONG, SPREAD, PASSED, SUMMED = range(1, 7)
 BEFORE = {
-    2: ((W_Q0, ACROSS), (W_P, START),),
-    3: ((W_Q0, RELAY), (W_Q2, START), (W_U0, START),),
+    2: ((W_Q0, ACROSS), (W_Q0, RELAY),),
+    3: ((W_Q2, START), (W_P, START), (W_U0, START),),
     5: ((W_Q0, BESIDE), (W_Q1, ACROSS),),
 }
 FORWARD = {
-    0: ((W_Q1, RELAY), (W_Q2, ACROSS), (W_P, ACROSS), (W_D0, START), (W_U1, START),),
-    4: ((W_Q1, BESIDE), (W_U0, ACROSS),),
-    6: ((W_Q2, RELAY), (W_P, RELAY),),
-    8: ((W_D0, ACROSS), (W_D1, START),),
-    9: ((W_D2, START),),
-    11: ((W_Q2, BESIDE), (W_U0, RELAY),),
-    13: ((W_U1, ACROSS),),
-    14: ((W_U2, START),),
-    15: ((W_P, BESIDE), (W_D0, RELAY),),
-    17: ((W_D1, ACROSS),),
-    19: ((W_U0, BESIDE), (W_U1, RELAY),),
+    0: ((W_Q1, RELAY), (W_Q2, ACROSS), (W_P, ACROSS), (W_D0, START),),
+    4: ((W_Q1, BESIDE),),
+    5: ((W_U0, ACROSS),),
+    6: ((W_Q2, RELAY), (W_D1, START),),
+    7: ((W_P, RELAY),),
+    8: ((W_U1, START),),
+    9: ((W_D0, ACROSS),),
+    10: ((W_U0, RELAY),),
+    11: ((W_Q2, BESIDE),),
+    14: ((W_D0, RELAY), (W_U2, START),),
+    15: ((W_D1, ACROSS),),
+    16: ((W_P, BESIDE), (W_D2, START),),
+    19: ((W_U1, ACROSS),),
+    20: ((W_U0, BESIDE), (W_D0, BESIDE),),
 }
 MIDDLE = {
-    0: ((W_D0, BESIDE),),
-    1: ((W_D1, RELAY), (W_U2, ACROSS), (W_D2, ACROSS),),
+    0: ((W_U2, ACROSS),),
+    1: ((W_D1, RELAY),),
+    2: ((W_U1, RELAY), (W_D2, ACROSS),),
 }
 TILE_STEP = {
-    0: ((W_U1, BESIDE),),
-    1: ((W_D1, BESIDE), (W_U2, RELAY), (W_D2, RELAY),),
-    2: ((W_U2, BESIDE), (W_D2, BESIDE),),
-    3: ((G_D0, FIRST), (G_U0, FIRST),),
+    1: ((W_U1, BESIDE), (W_D1, BESIDE), (W_U2, RELAY),),
+    2: ((W_D2, RELAY),),
+    3: ((G_D0, FIRST), (G_U0, FIRST), (W_U2, BESIDE), (W_D2, BESIDE),),
     5: ((G_D0, SECOND), (G_U0, SECOND), (G_D1, FIRST), (G_U1, FIRST),),
 }
 AFTER_TILES = {
-    1: ((G_D0, ALONG),),
-    2: ((G_D2, FIRST), (G_U2, FIRST),),
+    0: ((G_D0, ALONG),),
+    2: ((G_U0, ALONG), (G_D2, FIRST), (G_U2, FIRST),),
 }
 BACKWARD = {
-    1: ((G_D1, SECOND), (G_U1, SECOND),),
-    2: ((G_D0, SPREAD), (G_U0, ALONG),),
-    4: ((G_P, FIRST),),
-    7: ((G_D0, PASSED), (G_D2, SECOND),),
-    8: ((G_D1, ALONG), (G_U2, SECOND),),
-    9: ((G_U1, ALONG),),
-    10: ((G_Q0, FIRST),),
-    11: ((G_U0, SPREAD),),
+    1: ((G_U1, SECOND),),
+    3: ((G_D0, SPREAD), (G_D1, SECOND), (G_P, FIRST),),
+    5: ((G_D2, SECOND),),
+    7: ((G_U0, SPREAD), (G_U0, PASSED),),
+    9: ((G_D0, PASSED), (G_U1, ALONG), (G_Q0, FIRST),),
+    11: ((G_D1, ALONG),),
+    12: ((G_U2, SECOND),),
     14: ((G_D2, ALONG), (G_P, SECOND),),
-    15: ((G_Q0, SECOND),),
-    17: ((G_U0, PASSED), (G_D1, SPREAD), (G_D1, PASSED), (G_U1, SPREAD), (G_U1, PASSED), (G_Q1, FIRST),),
-    19: ((G_U2, ALONG),),
-    20: ((G_D0, SUMMED), (G_P, ALONG),),
+    16: ((G_U1, SPREAD), (G_Q0, SECOND),),
+    17: ((G_U0, SUMMED), (G_U2, ALONG),),
+    19: ((G_D1, SPREAD), (G_D1, PASSED), (G_Q1, FIRST),),
+    20: ((G_D2, SPREAD), (G_P, ALONG),),
 }
 LAST_STEPS = {
-    0: ((G_Q2, FIRST), (G_K2, FIRST), (G_V2, FIRST),),
-    1: ((G_D2, SPREAD), (G_Q2, SECOND),),
-    2: ((G_D2, PASSED), (G_P, SPREAD), (G_Q0, ALONG),),
-    3: ((G_U1, SUMMED), (G_Q1, SECOND),),
+    0: ((G_D0, SUMMED), (G_U2, SPREAD), (G_Q2, FIRST), (G_Q2, SECOND), (G_K2, FIRST),),
+    1: ((G_P, SPREAD), (G_Q0, ALONG), (G_V2, FIRST),),
+    3: ((G_U2, PASSED), (G_Q0, SPREAD),),
 }
 
 

time: 198 us -> 196 us (0.990)
  Pallas kernels: 196 us -> 194 us
    pallas_call x1, Pallas kernels: 182 us -> 180 us  [shards(): pl.pallas_call(functools.partial(layer_kernel, windows), out_shape=[shape...]
where the time goes in v1:
time: 196 us
  Pallas kernels  194 us (99%)
    pallas_call x1, Pallas kernels, shards(): pl.pallas_call(functools.partial(layer_kernel, windows), out_shape=[shape...  180 us
    pallas_call x1, Pallas kernels, update(): pl.pallas_call(update_kernel, grid=(steps,), in_specs=specs, out_specs=ou...  13.8 us

profile of v1, /device:TPU:0, one launch (start us, length us, event | category | flops | bytes accessed | tf_op | source)
XLA Modules:
  0.0 195.5 jit_solution(16960809078236479643)
XLA Ops:
  1.3 180.2 %layer.1 = (bf16[1008,768]{1,0:T(8,128)(2,1)}, f32[1008,768]{1,0:T(8,128)}, bf16[3,3,96,256]{3,2,1,0:T(8,128)(2,1)}, bf16[96,768]{1,0:T(8,128)(2,1)}, bf16[3,96,...) custom-call(bf16[1008,768]{1,0:T(8,128)(2,1)} %bitcast.13, ...), custom_call_target="tpu_custom_call" | custom-call | tf_op jit(solution)/shard_map/layer/pallas_call | solution.py:1319
  181.5 13.8 %update.1 = (f32[96,2304]{1,0:T(8,128)}, f32[96,2304]{1,0:T(8,128)}, f32[96,2304]{1,0:T(8,128)}, bf16[96,2304]{1,0:T(8,128)(2,1)}, f32[96,768]{1,0:T(8,128)}, /*...) custom-call(bf16[3,3,96,256]{3,2,1,0:T(8,128)(2,1)} %get-tuple-eleme, ...), custom_call_target="tpu_custom_call" | custom-call | tf_op jit(solution)/shard_map/update/pallas_call | solution.py:1293
